TPU v7x, 512 devices: a whole 4x8x8 slice. The times are simulated.
512 devices in a mesh: ctx: 64 (over z, x, core), head: 8 (over y).
Axes of the slice: x: 4, y: 8, z: 8, core: 2. Of those that a mesh axis runs over, the one named last changes fastest.
Arguments:
- tokens: bfloat16 [2, 16, 8192], P(None, None, 'ctx'), may hold values from -6 to 6
- w_query: bfloat16 [8192, 8192], P('ctx', 'head'), may hold values from -0.0625 to 0.0625
- w_key: bfloat16 [8192, 1024], P('ctx', 'head'), may hold values from -0.5 to 0.5
- w_value: bfloat16 [8192, 1024], P('ctx', 'head'), may hold values from -0.125 to 0.125
- key_cache: bfloat16 [2, 8, 131072, 128], P(None, 'head', 'ctx'), may hold values from -180 to 180
- value_cache: bfloat16 [2, 8, 131072, 128], P(None, 'head', 'ctx'), may hold values from -6 to 6
- lengths: int32 [2], replicated, may hold values from 65536 to 131072, as said below
- w_out: bfloat16 [8192, 8192], P('head', 'ctx'), may hold values from -0.1875 to 0.1875
Outputs:
- mixed: bfloat16 [2, 16, 8192], P(None, None, ('ctx', 'head'))
Inputs may be any that keep to these rules, and one draw needn't show every extreme that they name: `lengths`: every row's length is at least 65536, and one row's is exactly 131072.
All inputs are finite; a program needn't handle non-finite values.
Results may differ from a plain program's by a relative error of at most 0.015.
The roundings to bfloat16 on the way count: a program that leaves them out, or rounds other values in their place, can miss the bound.
Values may be sent and summed in bfloat16 or wider, within the bound.
A program may use at most 64 MiB of HBM per device.

v0:
```python
import math

import jax
import jax.numpy as jnp
from jax import lax
from jax.sharding import PartitionSpec as P


def per_device(tokens, w_query, w_key, w_value, key_cache, value_cache, lengths, w_out):
    row_count, draft_count, local_width = tokens.shape
    kv_local = key_cache.shape[1]
    slot_count = key_cache.shape[2]
    head_dim = key_cache.shape[3]
    group_size = w_query.shape[1] // (kv_local * head_dim)
    score_scale = 1.0 / math.sqrt(head_dim)
    flattened = tokens.reshape(row_count * draft_count, local_width)
    partials = (
        jnp.dot(flattened, w_query, preferred_element_type=jnp.float32),
        jnp.dot(flattened, w_key, preferred_element_type=jnp.float32),
        jnp.dot(flattened, w_value, preferred_element_type=jnp.float32),
    )
    query_sum, key_sum, value_sum = lax.psum((partials[0], partials[1], partials[2]), "ctx")
    query = (
        (query_sum * score_scale)
        .astype(jnp.bfloat16)
        .reshape(row_count, draft_count, kv_local, group_size, head_dim)
    )
    new_key = key_sum.reshape(row_count, draft_count, kv_local, head_dim)
    new_value = value_sum.reshape(row_count, draft_count, kv_local, head_dim)
    scores = jnp.einsum("btgqd,bgjd->bgqtj", query, key_cache, preferred_element_type=jnp.float32)
    offset_start = lax.axis_index("ctx") * slot_count
    slot_index = offset_start + jnp.arange(slot_count, dtype=jnp.int32)
    is_live = (slot_index[None, :] < lengths[:, None])[:, None, None, None, :]
    masked = jnp.where(is_live, scores, -1e30)
    local_max = masked.max(axis=-1)
    weights_local = jnp.where(is_live, jnp.exp(masked - local_max[..., None]), 0.0)
    local_sum = weights_local.sum(axis=-1)
    local_out = jnp.einsum(
        "bgqtj,bgjd->bgqtd",
        weights_local,
        value_cache.astype(jnp.float32),
        preferred_element_type=jnp.float32,
        precision=lax.Precision.HIGHEST,
    )
    total_max = lax.pmax(local_max, "ctx")
    factor = jnp.exp(local_max - total_max)
    total_sum, total_out = lax.psum((local_sum * factor, local_out * factor[..., None]), "ctx")
    draft_scores = jnp.einsum(
        "btgqd,bugd->bgqtu",
        query.astype(jnp.float32),
        new_key,
        preferred_element_type=jnp.float32,
        precision=lax.Precision.HIGHEST,
    )
    causal_mask = jnp.arange(draft_count)[:, None] >= jnp.arange(draft_count)[None, :]
    draft_scores = jnp.where(causal_mask, draft_scores, -1e30)
    top_score = jnp.maximum(total_max, draft_scores.max(axis=-1))
    cache_factor = jnp.exp(total_max - top_score)
    draft_weights = jnp.where(causal_mask, jnp.exp(draft_scores - top_score[..., None]), 0.0)
    denominator = total_sum * cache_factor + draft_weights.sum(axis=-1)
    numerator = total_out * cache_factor[..., None] + jnp.einsum(
        "bgqtu,bugd->bgqtd",
        draft_weights,
        new_value,
        preferred_element_type=jnp.float32,
        precision=lax.Precision.HIGHEST,
    )
    attended = (numerator / denominator[..., None]).astype(jnp.bfloat16)
    attended = attended.transpose(0, 3, 1, 2, 4).reshape(
        row_count * draft_count, kv_local * group_size * head_dim
    )
    projected = jnp.dot(attended, w_out, preferred_element_type=jnp.float32)
    summed = lax.psum(projected.astype(jnp.bfloat16), "head").astype(jnp.float32)
    piece_width = summed.shape[1] // lax.axis_size("head")
    result = lax.dynamic_slice_in_dim(summed, lax.axis_index("head") * piece_width, piece_width, 1)
    return result.astype(jnp.bfloat16).reshape(row_count, draft_count, result.shape[1])


def solution(mesh):
    return jax.shard_map(
        per_device,
        mesh=mesh,
        in_specs=(
            P(None, None, "ctx"),
            P("ctx", "head"),
            P("ctx", "head"),
            P("ctx", "head"),
            P(None, "head", "ctx", None),
            P(None, "head", "ctx", None),
            P(),
            P("head", "ctx"),
        ),
        out_specs=P(None, None, ("ctx", "head")),
        check_vma=False,
    )
```

profile of v0, /device:TPU:1, one launch (start us, length us, event | category | flops | bytes accessed | tf_op | source)
XLA Modules:
  0.0 726.8 jit_solution(17183836018537919685)
XLA Ops:
  6.5 0.0 copy-start
  6.5 0.0 all-reduce.4.cloned.1.call-start
  6.5 1.9 fusion.36
  8.4 0.0 all-reduce.4.cloned.1.call-update
  8.4 0.0 all-reduce.6.cloned.1.call-start
  8.5 0.9 fusion.38
  9.4 0.9 fusion.37
  10.3 0.7 broadcast_compare_fusion
  11.1 190.3 %all-reduce.4.cloned.1.call-done = f32[32,1024]{1,0:T(8,128)} async-done(((f32[32,1024]{1,0:T(8,128)}), f32[32,1024]{1,0:T(8,128)}) %all-reduce.4.cloned.1.call-update) | async-done | bytes 131088 | tf_op jit(solution)/shard_map/psum | solution.py:22
  201.4 0.9 fusion.22
  202.3 0.0 copy-done
  202.3 0.5 fusion.34
  202.9 241.7 %pmax.7 = f32[2,1,8,16]{2,3,0,1:T(8,128)S(1)} all-reduce(f32[2,1,8,16]{2,3,0,1:T(8,128)S(1)} %bitcast.119), channel_id=1, replica_groups=mesh['ctx'=64,'head'=8] {'ctx'}, use_global_device_ids=true, to_apply=%region_2.0 | all-reduce | flops 256 | bytes 2048 | tf_op jit(solution)/shard_map/pmax | solution.py:45
  444.6 0.0 copy-start.2
  444.6 0.5 fusion.4
  445.1 0.6 fusion.30
  445.7 0.1 copy-done.2
  445.8 2.2 fusion.8
  448.0 0.0 all-reduce.6.cloned.1.call-update
  448.0 246.2 %all-reduce = (f32[2,16,128]{2,1,0:T(8,128)S(1)}, f32[2,1,8,16]{2,3,0,1:T(8,128)S(1)}, f32[2,16,128]{2,1,0:T(8,128)S(1)}) all-reduce(f32[2,16,128]{2,1,0:T(8,128)S(1)} %bitcast.124, f32[2,1,8,16]{2,3,0,1:T(8,128)} %get-tuple-element.13, f32[2,16,128]{2,1,0:T(8,128)S(1)} %bitcast.123), channel_id=1, replica_groups=mesh['ctx'=64,'head'=8] {'ctx'}, use_global_device_ids=true, to_apply=%region_4.5 | all-reduce | flops 8448 | bytes 67584 | tf_op jit(solution)/shard_map/psum | solution.py:22
  694.2 0.6 fusion.35
  694.8 0.1 copy.35
  694.9 0.1 copy.36
  695.0 0.1 fusion.20
  695.0 0.1 copy.39
  695.1 0.1 copy.44
  695.2 0.0 all-reduce.6.cloned.1.call-done
  695.2 1.2 fusion.13
  696.4 0.0 copy-done.1
  696.4 0.3 convolution_convert_fusion
  696.7 22.6 %psum.47 = bf16[32,128]{0,1:T(8,128)(2,1)S(1)} all-reduce(bf16[32,128]{0,1:T(8,128)(2,1)S(1)} %convolution_convert_fusion), channel_id=1, replica_groups=mesh['ctx'=64,'head'=8] {'head'}, use_global_device_ids=true, to_apply=%region_10.11 | all-reduce | flops 4096 | bytes 16384 | tf_op jit(solution)/shard_map/psum | solution.py:73
  719.3 0.7 copy.48
  (7 shorter events, 0.0 us)
Async XLA Ops:
  6.5 195.8 %copy-start = (bf16[2,1,2048,128]{3,2,1,0:T(8,128)(2,1)S(1)}, bf16[2,1,2048,128]{3,2,1,0:T(8,128)(2,1)}, u32[]{:S(2)}) copy-start(bf16[2,1,2048,128]{3,2,1,0:T(8,128)(2,1)} %param.12) | copy-start | bytes 3145732
  6.5 194.8 %all-reduce.4.cloned.1.call-start = ((), (), s32[]{:S(2)}) async-start(), calls=%async_computation | async-start | bytes 262144 | tf_op jit(solution)/shard_map/psum | solution.py:22
  8.4 686.8 %all-reduce.6.cloned.1.call-start = ((), (), s32[]{:S(2)}) async-start(), calls=%async_computation.1 | async-start | bytes 262144 | tf_op jit(solution)/shard_map/psum | solution.py:47
  444.6 1.2 copy-start.2
  445.8 250.6 %copy-start.1 = (bf16[1024,128]{1,0:T(8,128)(2,1)S(1)}, bf16[1024,128]{1,0:T(8,128)(2,1)}, u32[]{:S(2)}) copy-start(bf16[1024,128]{1,0:T(8,128)(2,1)} %param.15) | copy-start | bytes 786436
Sparse Core Ops, SparseCore 0:
  10.8 190.5 all-reduce.3
  448.1 186.7 all-reduce.5
where the time goes:
time: 737 us; the launch traced here: 727 us
  blocking collectives  511 us (69%)
  waiting for transfers between devices  190 us (26%)
  between operations  13.5 us (2%)
  matrix products  8.39 us (1%)
    psum x1, blocking collectives, per_device(): lax.psum((partials[0], partials[1], partials[2]), 'ctx')  246 us
    pmax x1, blocking collectives, per_device(): total_max = lax.pmax(local_max, 'ctx')  242 us
    psum x1, waiting for transfers between devices, per_device(): lax.psum((partials[0], partials[1], partials[2]), 'ctx')  190 us
    psum x1, blocking collectives, per_device(): lax.psum(projected.astype(jnp.bfloat16), 'head').astype(jnp.float32)  22.6 us
  transfers between devices with their start and end apart: 2, of which 1 were waited for; matrix products, arithmetic and copies ran while one was open for 0% of the time, Pallas kernels for 0%

commit v1 on v0

v1 whole, which is shorter than its diff:
```python
import functools
import math

import jax
import jax.numpy as jnp
from jax import lax
from jax.experimental import pallas as pl
from jax.experimental.pallas import tpu as pltpu
from jax.sharding import PartitionSpec as P

F32, BF16 = jnp.float32, jnp.bfloat16
MESH = pl.DeviceIdType.MESH
NX = 4
NEG = -1e30


def dot_t(a, b, **kw):
    return lax.dot_general(a, b, (((1,), (1,)), ((), ())), preferred_element_type=F32, **kw)


def kernel(NZ, NY, slots,
           tok, wq, wk, wv, kc, vc, ln, wo, out,
           tok_v, wq_v, wk_v, wv_v, kc_v, vc_v, ln_s, wo_v, vt,
           p_other, p_own, r_core, s_x, r_x, s_z, r_zq, r_zkv, q_full, kv_full,
           s_buf, o_other, o_own, r_core2, s_x2, s_xml, r_x2, r_xml, s_z2, s_zml, r_z2, r_zml,
           o_draft, att, y_buf, s_y, r_y,
           load_sem, send_sem, recv_sem):
    ctx, y = lax.axis_index("ctx"), lax.axis_index("head")
    c = lax.rem(ctx, 2)
    x = lax.rem(ctx // 2, NX)
    z = ctx // (2 * NX)
    o = 1 - c

    def load(i, src, dst):
        cp = pltpu.make_async_copy(src, dst, load_sem.at[i])
        cp.start()
        return cp

    ld_tok = load(0, tok, tok_v)
    ld_wq = load(1, wq, wq_v)
    ld_wk = load(2, wk, wk_v)
    ld_wv = load(3, wv, wv_v)
    ld_vc = load(4, vc.at[:, 0], vc_v)
    ld_kc = load(5, kc.at[:, 0], kc_v)
    ld_wo = load(6, wo, wo_v)
    ld_ln = load(7, ln, ln_s)

    core_peer = {"ctx": ctx + 1 - 2 * c}
    x_peers = [(k, lax.rem(x + k, NX)) for k in (2, 1, 3)]
    x_dev = [{"ctx": (z * NX + xp) * 2 + c} for _, xp in x_peers]
    z_off = sorted(range(1, NZ), key=lambda k: -min(k, NZ - k))
    z_dev = [{"ctx": (lax.rem(z + k, NZ) * NX + x) * 2 + c} for k in z_off]
    y_off = sorted(range(1, NY), key=lambda k: -min(k, NY - k))
    y_dev = [{"head": lax.rem(y + k, NY)} for k in y_off]

    bar = pltpu.get_barrier_semaphore()
    everyone = z_dev + y_dev + x_dev + [core_peer]
    for d in everyone:
        pl.semaphore_signal(bar, inc=1, device_id=d, device_id_type=MESH)

    pending = []

    def send(ph, src, dst, dev):
        cp = pltpu.make_async_remote_copy(src_ref=src, dst_ref=dst, send_sem=send_sem.at[ph],
                                          recv_sem=recv_sem.at[ph], device_id=dev, device_id_type=MESH)
        cp.start()

    def arrive(ph, ref):
        pltpu.make_async_copy(ref, ref, recv_sem.at[ph]).wait()
        pending.append((ph, ref))

    def project(b, dst):
        t = tok_v[b]
        q = jnp.dot(t, wq_v[...], preferred_element_type=F32)
        k = jnp.dot(t, wk_v[...], preferred_element_type=F32)
        v = jnp.dot(t, wv_v[...], preferred_element_type=F32)
        for r in range(2):
            rows = slice(8 * r, 8 * r + 8)
            for ch, kv in ((0, k), (1, v)):
                dst[2 * r + ch, :, 0:512] = q[rows, 512 * ch:512 * ch + 512]
                dst[2 * r + ch, :, 512:640] = kv[rows]

    for cp in (ld_tok, ld_wq, ld_wk, ld_wv):
        cp.wait()
    project(o, p_other)
    pl.semaphore_wait(bar, len(everyone))
    send(0, p_other, r_core, core_peer)
    project(c, p_own)
    arrive(0, r_core)

    for i, (k, xp) in enumerate(x_peers):
        s_x[i] = p_own[xp] + r_core[xp]
        send(1, s_x.at[i], r_x.at[i], x_dev[i])
    mine = p_own[x] + r_core[x]
    arrive(1, r_x)
    for i in range(NX - 1):
        mine = mine + r_x[i]
    s_z[...] = mine
    for i in range(NZ - 1):
        send(2, s_z.at[:, 0:512], r_zq.at[i], z_dev[i])
    for i in range(NZ - 1):
        send(3, s_z.at[:, 512:640], r_zkv.at[i], z_dev[i])

    ld_vc.wait()
    for b in range(2):
        for i in range(4):
            vt[b, 0:128, 512 * i:512 * i + 512] = vc_v[b, 512 * i:512 * i + 512].T
        vt[b, 128:144] = jnp.ones((16, vt.shape[2]), BF16)
    ld_kc.wait()
    ld_ln.wait()

    qs = mine[:, 0:512]
    if NZ > 1:
        arrive(2, r_zq)
        for i in range(NZ - 1):
            qs = qs + r_zq[i]
    qs = jnp.concatenate([qs[:, 128 * i:128 * i + 128] for i in range(4)], axis=0)
    q_full[c, x] = (qs * (1.0 / math.sqrt(128.0))).astype(BF16)
    for i in range(NX - 1):
        send(4, q_full.at[c, x], q_full.at[c, x], x_dev[i])
    kvs = mine[:, 512:640]
    if NZ > 1:
        arrive(3, r_zkv)
        for i in range(NZ - 1):
            kvs = kvs + r_zkv[i]
    kv_full[x] = kvs
    for i in range(NX - 1):
        send(5, kv_full.at[x], kv_full.at[x], x_dev[i])
    arrive(4, q_full.at[0, 0:NX - 1])
    send(6, q_full.at[c], q_full.at[c], core_peer)
    arrive(6, q_full.at[0])

    n_pos = kc_v.shape[1]
    step = 512

    def attend(b, dst):
        q = q_full[b].reshape(128, 128)
        live = ln_s[b] - ctx * n_pos
        m = jnp.full((8, 128), NEG, F32)
        for i in range(n_pos // step):
            s = dot_t(kc_v[b, step * i:step * (i + 1)], q)
            at = lax.broadcasted_iota(jnp.int32, (step, 128), 0) + step * i
            s = jnp.where(at < live, s, NEG)
            s_buf[step * i:step * (i + 1)] = s
            m = jnp.maximum(m, jnp.max(s.reshape(step // 8, 8, 128), axis=0))
        m = jnp.max(m, axis=0, keepdims=True)
        acc = jnp.zeros((144, 128), F32)
        for i in range(n_pos // step):
            w = jnp.exp(s_buf[step * i:step * (i + 1)] - m).astype(BF16)
            acc = acc + jnp.dot(vt[b, :, step * i:step * (i + 1)], w, preferred_element_type=F32)
        dst[0:128] = acc[0:128]
        dst[128:129] = m
        dst[129:130] = acc[128:129]

    attend(o, o_other)
    send(7, o_other, r_core2, core_peer)
    attend(c, o_own)
    arrive(7, r_core2)

    m1, m2 = o_own[128:129], r_core2[128:129]
    top = jnp.maximum(m1, m2)
    f1, f2 = jnp.exp(m1 - top), jnp.exp(m2 - top)
    total = f1 * o_own[129:130] + f2 * r_core2[129:130]
    s_xml[0:1] = top
    s_xml[1:2] = total

    def chunk(xp):
        rows = pl.ds(pl.multiple_of(xp * 32, 32), 32)
        return f1 * o_own[rows] + f2 * r_core2[rows]

    for i, (k, xp) in enumerate(x_peers):
        s_x2[i] = chunk(xp).astype(BF16)
        send(8, s_x2.at[i], r_x2.at[i], x_dev[i])
        send(9, s_xml, r_xml.at[i], x_dev[i])
    part = chunk(x)

    arrive(5, kv_full.at[0:NX - 1])
    new_k = jnp.concatenate([kv_full[0], kv_full[2]], axis=0)
    new_v = jnp.concatenate([kv_full[1], kv_full[3]], axis=0)
    ds = dot_t(new_k, q_full[c].reshape(128, 128).astype(F32), precision=lax.Precision.HIGHEST)
    lane = lax.broadcasted_iota(jnp.int32, (16, 128), 1)
    u = lax.broadcasted_iota(jnp.int32, (16, 128), 0)
    ds = jnp.where(u <= (lane // 64) * 8 + lane % 8, ds, NEG)
    dm = jnp.max(ds, axis=0, keepdims=True)
    dw = jnp.exp(ds - dm)
    dl = jnp.sum(dw, axis=0, keepdims=True)
    o_draft[...] = lax.dot_general(new_v, dw, (((0,), (0,)), ((), ())), preferred_element_type=F32,
                                   precision=lax.Precision.HIGHEST)
    d_part = o_draft[pl.ds(pl.multiple_of(x * 32, 32), 32)]

    def combine(parts):
        top = functools.reduce(jnp.maximum, [m for m, _, _ in parts])
        tot, acc = 0.0, 0.0
        for m, l, a in parts:
            f = jnp.exp(m - top)
            tot = tot + f * l
            acc = acc + f * a
        return top, tot, acc

    arrive(8, r_x2)
    arrive(9, r_xml)
    top, total, part = combine(
        [(top, total, part)]
        + [(r_xml[i, 0:1], r_xml[i, 1:2], r_x2[i].astype(F32)) for i in range(NX - 1)])
    s_z2[...] = part.astype(BF16)
    s_zml[0:1] = top
    s_zml[1:2] = total
    for i in range(NZ - 1):
        send(10, s_z2, r_z2.at[i], z_dev[i])
        send(11, s_zml, r_zml.at[i], z_dev[i])
    ld_wo.wait()
    if NZ > 1:
        arrive(10, r_z2)
        arrive(11, r_zml)
    _, total, part = combine(
        [(top, total, part), (dm, dl, d_part)]
        + [(r_zml[i, 0:1], r_zml[i, 1:2], r_z2[i].astype(F32)) for i in range(NZ - 1)])
    att[c, x] = (part / total).astype(BF16)
    for i in range(NX - 1):
        send(12, att.at[c, x], att.at[c, x], x_dev[i])
    arrive(12, att.at[0, 0:NX - 1])
    send(13, att.at[c], att.at[c], core_peer)

    def mix(b):
        a = att[b].reshape(128, 128).astype(F32).T
        a = jnp.concatenate(
            [jnp.concatenate([a[64 * r + 8 * h:64 * r + 8 * h + 8] for h in range(8)], axis=1) for r in range(2)],
            axis=0)
        y_buf[b] = jnp.dot(a.astype(BF16), wo_v[...], preferred_element_type=F32)

    mix(c)
    arrive(13, att.at[0])
    mix(o)
    yt = y_buf[...].reshape(32, 128).T.astype(BF16)
    s_y[...] = yt.reshape(s_y.shape)
    for i in range(NY - 1):
        send(14, s_y.at[y_dev[i]["head"]], r_y.at[i], y_dev[i])
    ys = s_y[y].astype(F32)
    if NY > 1:
        arrive(14, r_y)
        for i in range(NY - 1):
            ys = ys + r_y[i].astype(F32)
    out[...] = ys.T.astype(BF16).reshape(out.shape)

    for ph, ref in pending:
        pltpu.make_async_copy(ref, ref, send_sem.at[ph]).wait()


def per_device(NZ, NY, *args):
    tok, wq, wk, wv, kc, vc, ln, wo = args
    n_pos, piece = kc.shape[2], wo.shape[1] // NY
    nz, ny = max(NZ - 1, 1), max(NY - 1, 1)
    V = pltpu.VMEM
    scratch = [
        V(tok.shape, BF16), V(wq.shape, BF16), V(wk.shape, BF16), V(wv.shape, BF16),
        V((2, n_pos, 128), BF16), V((2, n_pos, 128), BF16), pltpu.SMEM((2,), jnp.int32), V(wo.shape, BF16),
        V((2, 144, n_pos), BF16),
        V((4, 8, 640), F32), V((4, 8, 640), F32), V((4, 8, 640), F32),
        V((3, 8, 640), F32), V((3, 8, 640), F32), V((8, 640), F32), V((nz, 8, 512), F32), V((nz, 8, 128), F32),
        V((2, 4, 32, 128), BF16), V((4, 8, 128), F32),
        V((n_pos, 128), F32), V((136, 128), F32), V((136, 128), F32), V((136, 128), F32),
        V((3, 32, 128), BF16), V((2, 128), F32), V((3, 32, 128), BF16), V((3, 2, 128), F32),
        V((32, 128), BF16), V((2, 128), F32), V((nz, 32, 128), BF16), V((nz, 2, 128), F32),
        V((128, 128), F32), V((2, 4, 32, 128), BF16), V((2, 16, 128), F32),
        V((NY, piece, 32), BF16), V((ny, piece, 32), BF16),
        pltpu.SemaphoreType.DMA((8,)), pltpu.SemaphoreType.DMA((15,)), pltpu.SemaphoreType.DMA((15,)),
    ]
    return pl.pallas_call(
        functools.partial(kernel, NZ, NY, None),
        out_shape=jax.ShapeDtypeStruct((2, 16, piece), BF16),
        in_specs=[pl.BlockSpec(memory_space=pl.ANY)] * 8,
        out_specs=pl.BlockSpec(memory_space=pltpu.VMEM),
        scratch_shapes=scratch,
        compiler_params=pltpu.CompilerParams(
            collective_id=0, has_side_effects=True, vmem_limit_bytes=40 * 2**20),
        name="decode_step",
    )(*args)


def solution(mesh):
    NZ = mesh.shape["ctx"] // (2 * NX)
    return jax.shard_map(
        functools.partial(per_device, NZ, mesh.shape["head"]),
        mesh=mesh,
        in_specs=(
            P(None, None, "ctx"),
            P("ctx", "head"),
            P("ctx", "head"),
            P("ctx", "head"),
            P(None, "head", "ctx", None),
            P(None, "head", "ctx", None),
            P(),
            P("head", "ctx"),
        ),
        out_specs=P(None, None, ("ctx", "head")),
        check_vma=False,
    )
```

time: 737 us -> 57.7 us (0.08); the launches traced: 727 us -> 57.3 us
  blocking collectives: 511 us -> 0 us
  waiting for transfers between devices: 190 us -> 0 us
  Pallas kernels: 0 us -> 49.4 us
  between operations: 13.5 us -> 0.02 us
  matrix products: 8.39 us -> 0 us
    psum x2 -> x0, blocking collectives: 269 us -> none  [the longest x1 246 us: per_device(): lax.psum((partials[0], partials[1], partials[2]), 'ctx')]
    pmax x1 -> x0, blocking collectives: 242 us -> none  [per_device(): total_max = lax.pmax(local_max, 'ctx')]
    psum x2 -> x0, waiting for transfers between devices: 190 us -> none  [the longest x1 190 us: per_device(): lax.psum((partials[0], partials[1], partials[2]), 'ctx')]
    pallas_call x0 -> x1, Pallas kernels: none -> 49.4 us  [per_device(): pl.pallas_call(functools.partial(kernel, NZ, NY, None), out_shape=jax.Sha...]
    dot_general x8 -> x0, matrix products: 8.39 us -> none  [the longest x1 2.17 us: per_device(): jnp.einsum('bgqtj,bgjd->bgqtd', weights_local, value_cache.astype(jnp.flo...]
    unnamed x7 -> x17, local copies, waits for them, and re-layouts: 0.13 us -> 7.81 us
  transfers between devices with their start and end apart: 2 -> 0, of which waited for: 1 -> 0; matrix products, arithmetic and copies ran while one was open for 0% -> 0% of each run, Pallas kernels for 0% -> 0%
where the time goes in v1:
time: 57.7 us; the launch traced here: 57.3 us
  Pallas kernels  49.4 us (86%)
  local copies, waits for them, and re-layouts  7.81 us (14%)
    pallas_call x1, Pallas kernels, per_device(): pl.pallas_call(functools.partial(kernel, NZ, NY, None), out_shape=jax.Sha...  49.4 us
    unnamed x17, local copies, waits for them, and re-layouts  7.81 us

profile of v1, /device:TPU:1, one launch (start us, length us, event | category | flops | bytes accessed | tf_op | source)
XLA Modules:
  0.0 57.3 jit_solution(17664990936434150043)
XLA Ops:
  0.0 0.0 copy-start
  0.0 1.2 %copy-done = bf16[2,1,2048,128]{3,2,1,0:T(8,128)(2,1)S(1)} copy-done((bf16[2,1,2048,128]{3,2,1,0:T(8,128)(2,1)S(1)}, bf16[2,1,2048,128]{3,2,1,0:T(8,128)(2,1)}, u32[]{:S(2)}) %copy-start) | copy-done | bytes 1048600
  1.2 0.0 copy-start.1
  1.2 1.2 %copy-done.1 = bf16[2,1,2048,128]{3,2,1,0:T(8,128)(2,1)S(1)} copy-done((bf16[2,1,2048,128]{3,2,1,0:T(8,128)(2,1)S(1)}, bf16[2,1,2048,128]{3,2,1,0:T(8,128)(2,1)}, u32[]{:S(2)}) %copy-start.1) | copy-done | bytes 1048600
  2.5 0.0 copy-start.2
  2.5 0.9 %copy-done.2 = bf16[128,1024]{1,0:T(8,128)(2,1)S(1)} copy-done((bf16[128,1024]{1,0:T(8,128)(2,1)S(1)}, bf16[128,1024]{1,0:T(8,128)(2,1)}, u32[]{:S(2)}) %copy-start.2) | copy-done | bytes 262168
  3.4 0.0 copy-start.3
  3.4 0.9 %copy-done.3 = bf16[1024,128]{1,0:T(8,128)(2,1)S(1)} copy-done((bf16[1024,128]{1,0:T(8,128)(2,1)S(1)}, bf16[1024,128]{1,0:T(8,128)(2,1)}, u32[]{:S(2)}) %copy-start.3) | copy-done | bytes 262168
  4.4 0.0 copy-start.4
  4.4 0.8 %copy-done.4 = bf16[128,128]{1,0:T(8,128)(2,1)S(1)} copy-done((bf16[128,128]{1,0:T(8,128)(2,1)S(1)}, bf16[128,128]{1,0:T(8,128)(2,1)}, u32[]{:S(2)}) %copy-start.4) | copy-done | bytes 32792
  5.1 0.0 copy-start.5
  5.1 0.8 %copy-done.5 = bf16[128,128]{1,0:T(8,128)(2,1)S(1)} copy-done((bf16[128,128]{1,0:T(8,128)(2,1)S(1)}, bf16[128,128]{1,0:T(8,128)(2,1)}, u32[]{:S(2)}) %copy-start.5) | copy-done | bytes 32792
  5.9 0.0 copy-start.6
  5.9 0.7 %copy-done.6 = bf16[2,16,128]{2,1,0:T(8,128)(2,1)S(1)} copy-done((bf16[2,16,128]{2,1,0:T(8,128)(2,1)S(1)}, bf16[2,16,128]{2,1,0:T(8,128)(2,1)}, u32[]{:S(2)}) %copy-start.6) | copy-done | bytes 8216
  6.6 0.0 copy-start.7
  6.6 0.7 %copy-done.7 = s32[2]{0:T(128)S(1)} copy-done((s32[2]{0:T(128)S(1)}, s32[2]{0:T(128)}, u32[]{:S(2)}) %copy-start.7) | copy-done | bytes 32
  7.2 49.4 %decode_step.1 = bf16[2,16,16]{2,1,0:T(8,128)(2,1)S(1)} custom-call(bf16[2,16,128]{2,1,0:T(8,128)(2,1)S(1)} %copy-done.6, bf16[128,1024]{1,0:T(8,128)(2,1)S(1)} %copy-done.2, bf16[128,128]{1,0:T(8,128)(2,1)S(1)} %copy-done.4, bf16[128,128]{1,0:T(8,128)(2,1)S(1)} %copy-done.5, bf16[2,1,2048,128]{3,2,1,0:T(8,128)(2,1)S(1)} %copy-done, ...), custom_call_target="tpu_custom_call" | custom-call | tf_op jit(solution)/shard_map/decode_step/pallas_call | solution.py:268
  56.7 0.6 %copy.10 = bf16[2,16,16]{2,1,0:T(8,128)(2,1)} copy(bf16[2,16,16]{2,1,0:T(8,128)(2,1)S(1)} %decode_step.1) | data formatting | bytes 2048
Async XLA Ops:
  0.0 1.2 %copy-start = (bf16[2,1,2048,128]{3,2,1,0:T(8,128)(2,1)S(1)}, bf16[2,1,2048,128]{3,2,1,0:T(8,128)(2,1)}, u32[]{:S(2)}) copy-start(bf16[2,1,2048,128]{3,2,1,0:T(8,128)(2,1)} %kc.1) | copy-start | bytes 3145732
  1.2 1.2 %copy-start.1 = (bf16[2,1,2048,128]{3,2,1,0:T(8,128)(2,1)S(1)}, bf16[2,1,2048,128]{3,2,1,0:T(8,128)(2,1)}, u32[]{:S(2)}) copy-start(bf16[2,1,2048,128]{3,2,1,0:T(8,128)(2,1)} %vc.1) | copy-start | bytes 3145732
  2.5 0.9 %copy-start.2 = (bf16[128,1024]{1,0:T(8,128)(2,1)S(1)}, bf16[128,1024]{1,0:T(8,128)(2,1)}, u32[]{:S(2)}) copy-start(bf16[128,1024]{1,0:T(8,128)(2,1)} %wq.1) | copy-start | bytes 786436
  3.4 0.9 %copy-start.3 = (bf16[1024,128]{1,0:T(8,128)(2,1)S(1)}, bf16[1024,128]{1,0:T(8,128)(2,1)}, u32[]{:S(2)}) copy-start(bf16[1024,128]{1,0:T(8,128)(2,1)} %wo.1) | copy-start | bytes 786436
  4.4 0.8 %copy-start.4 = (bf16[128,128]{1,0:T(8,128)(2,1)S(1)}, bf16[128,128]{1,0:T(8,128)(2,1)}, u32[]{:S(2)}) copy-start(bf16[128,128]{1,0:T(8,128)(2,1)} %wk.1) | copy-start | bytes 98308
  5.1 0.8 %copy-start.5 = (bf16[128,128]{1,0:T(8,128)(2,1)S(1)}, bf16[128,128]{1,0:T(8,128)(2,1)}, u32[]{:S(2)}) copy-start(bf16[128,128]{1,0:T(8,128)(2,1)} %wv.1) | copy-start | bytes 98308
  5.9 0.7 %copy-start.6 = (bf16[2,16,128]{2,1,0:T(8,128)(2,1)S(1)}, bf16[2,16,128]{2,1,0:T(8,128)(2,1)}, u32[]{:S(2)}) copy-start(bf16[2,16,128]{2,1,0:T(8,128)(2,1)} %tok.1) | copy-start | bytes 24580
  6.6 0.7 %copy-start.7 = (s32[2]{0:T(128)S(1)}, s32[2]{0:T(128)}, u32[]{:S(2)}) copy-start(s32[2]{0:T(128)} %ln.1) | copy-start | bytes 28

commit v2 on v1

--- a/solution.py
+++ b/solution.py
@@ -31,6 +31,19 @@
     z = ctx // (2 * NX)
     o = 1 - c
 
+    core_peer = {"ctx": ctx + 1 - 2 * c}
+    x_peers = [(k, lax.rem(x + k, NX)) for k in (2, 1, 3)]
+    x_dev = [{"ctx": (z * NX + xp) * 2 + c} for _, xp in x_peers]
+    z_off = sorted(range(1, NZ), key=lambda k: -min(k, NZ - k))
+    z_dev = [{"ctx": (lax.rem(z + k, NZ) * NX + x) * 2 + c} for k in z_off]
+    y_off = sorted(range(1, NY), key=lambda k: -min(k, NY - k))
+    y_dev = [{"head": lax.rem(y + k, NY)} for k in y_off]
+
+    bar = pltpu.get_barrier_semaphore()
+    everyone = z_dev + y_dev + x_dev + [core_peer]
+    for d in everyone:
+        pl.semaphore_signal(bar, inc=1, device_id=d, device_id_type=MESH)
+
     def load(i, src, dst):
         cp = pltpu.make_async_copy(src, dst, load_sem.at[i])
         cp.start()
@@ -44,19 +57,6 @@
     ld_kc = load(5, kc.at[:, 0], kc_v)
     ld_wo = load(6, wo, wo_v)
     ld_ln = load(7, ln, ln_s)
-
-    core_peer = {"ctx": ctx + 1 - 2 * c}
-    x_peers = [(k, lax.rem(x + k, NX)) for k in (2, 1, 3)]
-    x_dev = [{"ctx": (z * NX + xp) * 2 + c} for _, xp in x_peers]
-    z_off = sorted(range(1, NZ), key=lambda k: -min(k, NZ - k))
-    z_dev = [{"ctx": (lax.rem(z + k, NZ) * NX + x) * 2 + c} for k in z_off]
-    y_off = sorted(range(1, NY), key=lambda k: -min(k, NY - k))
-    y_dev = [{"head": lax.rem(y + k, NY)} for k in y_off]
-
-    bar = pltpu.get_barrier_semaphore()
-    everyone = z_dev + y_dev + x_dev + [core_peer]
-    for d in everyone:
-        pl.semaphore_signal(bar, inc=1, device_id=d, device_id_type=MESH)
 
     pending = []
 
@@ -272,7 +272,7 @@
         out_specs=pl.BlockSpec(memory_space=pltpu.VMEM),
         scratch_shapes=scratch,
         compiler_params=pltpu.CompilerParams(
-            collective_id=0, has_side_effects=True, vmem_limit_bytes=40 * 2**20),
+            collective_id=0, has_side_effects=True, vmem_limit_bytes=60 * 2**20),
         name="decode_step",
     )(*args)
 

time: 57.7 us -> 51.3 us (0.89)
  local copies, waits for them, and re-layouts: 7.81 us -> 1.3 us
    unnamed x17 -> x1, local copies, waits for them, and re-layouts: 7.81 us -> 1.3 us
where the time goes in v2:
time: 51.3 us; the launch traced here: 51.1 us
  Pallas kernels  49.8 us (97%)
  local copies, waits for them, and re-layouts  1.3 us (3%)
    pallas_call x1, Pallas kernels, per_device(): pl.pallas_call(functools.partial(kernel, NZ, NY, None), out_shape=jax.Sha...  49.8 us
    unnamed x1, local copies, waits for them, and re-layouts  1.3 us

profile of v2, /device:TPU:1, one launch (start us, length us, event | category | flops | bytes accessed | tf_op | source)
XLA Modules:
  0.0 51.1 jit_solution(17527914880054747364)
XLA Ops:
  0.0 49.8 %decode_step.1 = bf16[2,16,16]{2,1,0:T(8,128)(2,1)} custom-call(bf16[2,16,128]{2,1,0:T(8,128)(2,1)} %tok.1, bf16[128,1024]{1,0:T(8,128)(2,1)} %wq.1, bf16[128,128]{1,0:T(8,128)(2,1)} %wk.1, bf16[128,128]{1,0:T(8,128)(2,1)} %wv.1, bf16[2,1,2048,128]{3,2,1,0:T(8,128)(2,1)} %kc.1, bf16[2,1,2048,128]{3,2,1,0:T(8,128)(2,1)} %vc.1, s32[2]{0:T(128)} %ln.1, ...), custom_call_target="tpu_custom_call" | custom-call | tf_op jit(solution)/shard_map/decode_step/pallas_call | solution.py:268
  49.8 1.3 %copy.10 = bf16[2,16,16]{2,1,0:T(8,128)(2,1)} copy(bf16[2,16,16]{2,1,0:T(8,128)(2,1)} %decode_step.1) | data formatting | bytes 2048

commit v3 on v2

v3 whole, which is shorter than its diff:
```python
import functools
import math

import jax
import jax.numpy as jnp
from jax import lax
from jax.experimental import pallas as pl
from jax.experimental.pallas import tpu as pltpu
from jax.sharding import PartitionSpec as P

F32, BF16 = jnp.float32, jnp.bfloat16
MESH = pl.DeviceIdType.MESH
NX = 4
NEG = -1e30


def dot_t(a, b, **kw):
    return lax.dot_general(a, b, (((1,), (1,)), ((), ())), preferred_element_type=F32, **kw)


def kernel(NZ, NY,
           tok, wq, wk, wv, kc, vc, ln, wo, out,
           tok_v, wq_v, wk_v, wv_v, k_v, v_v, ln_s, wo_v, vt,
           p_oq, p_okv, p_cq, p_ckv, r_cq, r_ckv, s_zq, r_zq, s_xkv, r_xkv, r_xq, s_zkv, r_zkv, q_full, kv_full,
           s_buf, o_buf, s_x2, s_xml, r_x2, r_xml, s_z2, s_zml, r_z2, r_zml,
           o_draft, att, y_buf, s_y, r_y,
           load_sem, send_sem, recv_sem):
    ctx, y = lax.axis_index("ctx"), lax.axis_index("head")
    c = lax.rem(ctx, 2)
    x = lax.rem(ctx // 2, NX)
    z = ctx // (2 * NX)
    o = 1 - c
    n_pos, hz = k_v.shape[1], 8 // NZ

    core_peer = {"ctx": ctx + 1 - 2 * c}
    x_peers = [lax.rem(x + k, NX) for k in (2, 1, 3)]
    x_dev = [{"ctx": (z * NX + xp) * 2 + c} for xp in x_peers]
    z_peers = [lax.rem(z + k, NZ) for k in sorted(range(1, NZ), key=lambda k: -min(k, NZ - k))]
    z_dev = [{"ctx": (zp * NX + x) * 2 + c} for zp in z_peers]
    y_peers = [lax.rem(y + k, NY) for k in sorted(range(1, NY), key=lambda k: -min(k, NY - k))]
    y_dev = [{"head": yp} for yp in y_peers]

    bar = pltpu.get_barrier_semaphore()
    everyone = z_dev + y_dev + x_dev + [core_peer]
    for d in everyone:
        pl.semaphore_signal(bar, inc=1, device_id=d, device_id_type=MESH)

    def load(i, src, dst):
        cp = pltpu.make_async_copy(src, dst, load_sem.at[i])
        cp.start()
        return cp

    ld_tok = load(0, tok, tok_v)
    ld_wq = load(1, wq, wq_v)
    ld_wk = load(2, wk, wk_v)
    ld_wv = load(3, wv, wv_v)
    ld_v = load(4, vc.at[c, 0], v_v.at[0])
    ld_k = load(5, kc.at[c, 0], k_v.at[0])
    ld_wo = load(6, wo, wo_v)
    ld_ln = load(7, ln, ln_s)

    pending = []

    def send(ph, src, dst, dev):
        pltpu.make_async_remote_copy(src_ref=src, dst_ref=dst, send_sem=send_sem.at[ph],
                                     recv_sem=recv_sem.at[ph], device_id=dev, device_id_type=MESH).start()

    def arrive(ph, ref):
        pltpu.make_async_copy(ref, ref, recv_sem.at[ph]).wait()
        pending.append((ph, ref))

    def project(b, dst_q, dst_kv):
        t = tok_v[b]
        q = jnp.dot(t, wq_v[...], preferred_element_type=F32)
        k = jnp.dot(t, wk_v[...], preferred_element_type=F32)
        v = jnp.dot(t, wv_v[...], preferred_element_type=F32)
        for h in range(8):
            dst_q[h] = q[:, 128 * h:128 * h + 128]
        for r in range(2):
            dst_kv[2 * r] = k[8 * r:8 * r + 8]
            dst_kv[2 * r + 1] = v[8 * r:8 * r + 8]

    for cp in (ld_tok, ld_wq, ld_wk, ld_wv):
        cp.wait()
    project(o, p_oq, p_okv)
    project(c, p_cq, p_ckv)
    pl.semaphore_wait(bar, len(everyone))
    send(0, p_oq, r_cq, core_peer)
    send(1, p_okv, r_ckv, core_peer)

    arrive(0, r_cq)
    for i, zp in enumerate(z_peers):
        heads = pl.ds(zp * hz, hz)
        s_zq[i] = p_cq[heads] + r_cq[heads]
        send(2, s_zq.at[i], r_zq.at[i], z_dev[i])
    heads = pl.ds(z * hz, hz)
    qs = p_cq[heads] + r_cq[heads]

    arrive(1, r_ckv)
    for i, xp in enumerate(x_peers):
        s_xkv[i] = p_ckv[xp] + r_ckv[xp]
        send(3, s_xkv.at[i], r_xkv.at[i], x_dev[i])
    kvs = p_ckv[x] + r_ckv[x]

    send(8, vc.at[o, 0], v_v.at[1], core_peer)
    send(9, kc.at[o, 0], k_v.at[1], core_peer)

    if NZ > 1:
        arrive(2, r_zq)
        for i in range(NZ - 1):
            qs = qs + r_zq[i]
    r_xq[x] = qs
    for i in range(NX - 1):
        send(4, r_xq.at[x], r_xq.at[x], x_dev[i])

    arrive(3, r_xkv)
    for i in range(NX - 1):
        kvs = kvs + r_xkv[i]
    s_zkv[...] = kvs
    for i in range(NZ - 1):
        send(5, s_zkv, r_zkv.at[i], z_dev[i])

    arrive(4, r_xq.at[0:NX - 1])
    qs = (r_xq[0] + r_xq[1]) + (r_xq[2] + r_xq[3])
    q_full[heads] = (qs * (1.0 / math.sqrt(128.0))).astype(BF16)
    for i in range(NZ - 1):
        send(6, q_full.at[heads], q_full.at[heads], z_dev[i])

    if NZ > 1:
        arrive(5, r_zkv)
        for i in range(NZ - 1):
            kvs = kvs + r_zkv[i]
    kv_full[x] = kvs
    for i in range(NX - 1):
        send(7, kv_full.at[x], kv_full.at[x], x_dev[i])

    vt[128:144] = jnp.ones((16, vt.shape[1]), BF16)

    def transpose_values(half):
        for i in range(4):
            w = n_pos // 4
            vt[0:128, half * n_pos + w * i:half * n_pos + w * (i + 1)] = v_v[half, w * i:w * (i + 1)].T

    ld_v.wait()
    transpose_values(0)
    arrive(8, v_v.at[0])
    transpose_values(1)
    ld_k.wait()
    arrive(9, k_v.at[0])
    ld_ln.wait()
    if NZ > 1:
        arrive(6, q_full.at[0:8 - hz])

    q = q_full[...].reshape(128, 128)
    step = 512
    steps = [(half, i) for half in range(2) for i in range(n_pos // step)]
    m = jnp.full((8, 128), NEG, F32)
    for n, (half, i) in enumerate(steps):
        s = dot_t(k_v[half, step * i:step * (i + 1)], q)
        live = ln_s[c] - (ctx + half * (1 - 2 * c)) * n_pos - step * i
        s = jnp.where(lax.broadcasted_iota(jnp.int32, (step, 128), 0) < live, s, NEG)
        s_buf[step * n:step * (n + 1)] = s
        m = jnp.maximum(m, jnp.max(s.reshape(step // 8, 8, 128), axis=0))
    m = jnp.max(m, axis=0, keepdims=True)
    acc = jnp.zeros((144, 128), F32)
    for n in range(len(steps)):
        w = jnp.exp(s_buf[step * n:step * (n + 1)] - m).astype(BF16)
        acc = acc + jnp.dot(vt[:, step * n:step * (n + 1)], w, preferred_element_type=F32)
    total = acc[128:129]
    o_buf[...] = acc[0:128]
    s_xml[0:1] = m
    s_xml[1:2] = total

    def chunk(xp):
        return o_buf[pl.ds(pl.multiple_of(xp * 32, 32), 32)]

    for i, xp in enumerate(x_peers):
        s_x2[i] = chunk(xp).astype(BF16)
        send(10, s_x2.at[i], r_x2.at[i], x_dev[i])
        send(11, s_xml, r_xml.at[i], x_dev[i])
    part = chunk(x)

    arrive(7, kv_full.at[0:NX - 1])
    new_k = jnp.concatenate([kv_full[0], kv_full[2]], axis=0)
    new_v = jnp.concatenate([kv_full[1], kv_full[3]], axis=0)
    ds = dot_t(new_k, q.astype(F32), precision=lax.Precision.HIGHEST)
    lane = lax.broadcasted_iota(jnp.int32, (16, 128), 1)
    u = lax.broadcasted_iota(jnp.int32, (16, 128), 0)
    ds = jnp.where(u <= lane % 16, ds, NEG)
    dm = jnp.max(ds, axis=0, keepdims=True)
    dw = jnp.exp(ds - dm)
    dl = jnp.sum(dw, axis=0, keepdims=True)
    o_draft[...] = lax.dot_general(new_v, dw, (((0,), (0,)), ((), ())), preferred_element_type=F32,
                                   precision=lax.Precision.HIGHEST)
    d_part = o_draft[pl.ds(pl.multiple_of(x * 32, 32), 32)]

    def combine(parts):
        top = functools.reduce(jnp.maximum, [m for m, _, _ in parts])
        tot, acc = 0.0, 0.0
        for m, l, a in parts:
            f = jnp.exp(m - top)
            tot = tot + f * l
            acc = acc + f * a
        return top, tot, acc

    arrive(10, r_x2)
    arrive(11, r_xml)
    m, total, part = combine(
        [(m, total, part)] + [(r_xml[i, 0:1], r_xml[i, 1:2], r_x2[i].astype(F32)) for i in range(NX - 1)])
    s_z2[...] = part.astype(BF16)
    s_zml[0:1] = m
    s_zml[1:2] = total
    for i in range(NZ - 1):
        send(12, s_z2, r_z2.at[i], z_dev[i])
        send(13, s_zml, r_zml.at[i], z_dev[i])
    ld_wo.wait()
    if NZ > 1:
        arrive(12, r_z2)
        arrive(13, r_zml)
    _, total, part = combine(
        [(m, total, part), (dm, dl, d_part)]
        + [(r_zml[i, 0:1], r_zml[i, 1:2], r_z2[i].astype(F32)) for i in range(NZ - 1)])
    att[c, x] = (part / total).astype(BF16)
    for i in range(NX - 1):
        send(14, att.at[c, x], att.at[c, x], x_dev[i])
    arrive(14, att.at[0, 0:NX - 1])
    send(15, att.at[c], att.at[c], core_peer)

    def mix(b):
        a = att[b].reshape(128, 128).T
        a = jnp.concatenate([a[16 * h:16 * h + 16] for h in range(8)], axis=1)
        y_buf[b] = jnp.dot(a, wo_v[...], preferred_element_type=F32)

    mix(c)
    arrive(15, att.at[0])
    mix(o)
    yt = y_buf[...].reshape(32, 128).T.astype(BF16)
    s_y[...] = yt.reshape(s_y.shape)
    for i in range(NY - 1):
        send(16, s_y.at[y_peers[i]], r_y.at[i], y_dev[i])
    ys = s_y[y].astype(F32)
    if NY > 1:
        arrive(16, r_y)
        for i in range(NY - 1):
            ys = ys + r_y[i].astype(F32)
    out[...] = ys.T.astype(BF16).reshape(out.shape)

    for ph, ref in pending:
        pltpu.make_async_copy(ref, ref, send_sem.at[ph]).wait()


def per_device(NZ, NY, *args):
    tok, wq, wk, wv, kc, vc, ln, wo = args
    n_pos, piece, hz = kc.shape[2], wo.shape[1] // NY, 8 // NZ
    nz, ny = max(NZ - 1, 1), max(NY - 1, 1)
    V = pltpu.VMEM
    scratch = [
        V(tok.shape, BF16), V(wq.shape, BF16), V(wk.shape, BF16), V(wv.shape, BF16),
        V((2, n_pos, 128), BF16), V((2, n_pos, 128), BF16), pltpu.SMEM((2,), jnp.int32), V(wo.shape, BF16),
        V((144, 2 * n_pos), BF16),
        V((8, 16, 128), F32), V((4, 8, 128), F32), V((8, 16, 128), F32), V((4, 8, 128), F32),
        V((8, 16, 128), F32), V((4, 8, 128), F32),
        V((nz, hz, 16, 128), F32), V((nz, hz, 16, 128), F32), V((3, 8, 128), F32), V((3, 8, 128), F32),
        V((4, hz, 16, 128), F32), V((8, 128), F32), V((nz, 8, 128), F32),
        V((8, 16, 128), BF16), V((4, 8, 128), F32),
        V((2 * n_pos, 128), F32), V((128, 128), F32),
        V((3, 32, 128), BF16), V((2, 128), F32), V((3, 32, 128), BF16), V((3, 2, 128), F32),
        V((32, 128), BF16), V((2, 128), F32), V((nz, 32, 128), BF16), V((nz, 2, 128), F32),
        V((128, 128), F32), V((2, 4, 32, 128), BF16), V((2, 16, 128), F32),
        V((NY, piece, 32), BF16), V((ny, piece, 32), BF16),
        pltpu.SemaphoreType.DMA((8,)), pltpu.SemaphoreType.DMA((17,)), pltpu.SemaphoreType.DMA((17,)),
    ]
    return pl.pallas_call(
        functools.partial(kernel, NZ, NY),
        out_shape=jax.ShapeDtypeStruct((2, 16, piece), BF16),
        in_specs=[pl.BlockSpec(memory_space=pl.ANY)] * 8,
        out_specs=pl.BlockSpec(memory_space=pltpu.VMEM),
        scratch_shapes=scratch,
        compiler_params=pltpu.CompilerParams(
            collective_id=0, has_side_effects=True, vmem_limit_bytes=60 * 2**20),
        name="decode_step",
    )(*args)


def solution(mesh):
    NZ = mesh.shape["ctx"] // (2 * NX)
    return jax.shard_map(
        functools.partial(per_device, NZ, mesh.shape["head"]),
        mesh=mesh,
        in_specs=(
            P(None, None, "ctx"),
            P("ctx", "head"),
            P("ctx", "head"),
            P("ctx", "head"),
            P(None, "head", "ctx", None),
            P(None, "head", "ctx", None),
            P(),
            P("head", "ctx"),
        ),
        out_specs=P(None, None, ("ctx", "head")),
        check_vma=False,
    )
```

time: 51.3 us -> 49 us (0.955)
  Pallas kernels: 49.8 us -> 47.4 us
    pallas_call x1, Pallas kernels: 49.8 us -> 47.4 us  [per_device(): pl.pallas_call(functools.partial(kernel, NZ, NY), out_shape=jax.ShapeDtyp...]
where the time goes in v3:
time: 49 us; the launch traced here: 48.7 us
  Pallas kernels  47.4 us (97%)
  local copies, waits for them, and re-layouts  1.3 us (3%)
    pallas_call x1, Pallas kernels, per_device(): pl.pallas_call(functools.partial(kernel, NZ, NY), out_shape=jax.ShapeDtyp...  47.4 us
    unnamed x1, local copies, waits for them, and re-layouts  1.3 us

profile of v3, /device:TPU:1, one launch (start us, length us, event | category | flops | bytes accessed | tf_op | source)
XLA Modules:
  0.0 48.7 jit_solution(4520356097384111932)
XLA Ops:
  0.0 47.4 %decode_step.1 = bf16[2,16,16]{2,1,0:T(8,128)(2,1)} custom-call(bf16[2,16,128]{2,1,0:T(8,128)(2,1)} %tok.1, bf16[128,1024]{1,0:T(8,128)(2,1)} %wq.1, bf16[128,128]{1,0:T(8,128)(2,1)} %wk.1, bf16[128,128]{1,0:T(8,128)(2,1)} %wv.1, bf16[2,1,2048,128]{3,2,1,0:T(8,128)(2,1)} %kc.1, bf16[2,1,2048,128]{3,2,1,0:T(8,128)(2,1)} %vc.1, s32[2]{0:T(128)} %ln.1, ...), custom_call_target="tpu_custom_call" | custom-call | tf_op jit(solution)/shard_map/decode_step/pallas_call | solution.py:273
  47.4 1.3 %copy.10 = bf16[2,16,16]{2,1,0:T(8,128)(2,1)} copy(bf16[2,16,16]{2,1,0:T(8,128)(2,1)} %decode_step.1) | data formatting | bytes 2048

commit v4 on v3

--- a/solution.py
+++ b/solution.py
@@ -35,13 +35,14 @@
     core_peer = {"ctx": ctx + 1 - 2 * c}
     x_peers = [lax.rem(x + k, NX) for k in (2, 1, 3)]
     x_dev = [{"ctx": (z * NX + xp) * 2 + c} for xp in x_peers]
+    far_dev = [{"ctx": (z * NX + xp) * 2 + o} for xp in x_peers]
     z_peers = [lax.rem(z + k, NZ) for k in sorted(range(1, NZ), key=lambda k: -min(k, NZ - k))]
     z_dev = [{"ctx": (zp * NX + x) * 2 + c} for zp in z_peers]
     y_peers = [lax.rem(y + k, NY) for k in sorted(range(1, NY), key=lambda k: -min(k, NY - k))]
     y_dev = [{"head": yp} for yp in y_peers]
 
     bar = pltpu.get_barrier_semaphore()
-    everyone = z_dev + y_dev + x_dev + [core_peer]
+    everyone = z_dev + y_dev + far_dev + x_dev + [core_peer]
     for d in everyone:
         pl.semaphore_signal(bar, inc=1, device_id=d, device_id_type=MESH)
 
@@ -62,12 +63,12 @@
     pending = []
 
     def send(ph, src, dst, dev):
-        pltpu.make_async_remote_copy(src_ref=src, dst_ref=dst, send_sem=send_sem.at[ph],
+        pltpu.make_async_remote_copy(src_ref=src, dst_ref=dst, send_sem=send_sem,
                                      recv_sem=recv_sem.at[ph], device_id=dev, device_id_type=MESH).start()
 
     def arrive(ph, ref):
         pltpu.make_async_copy(ref, ref, recv_sem.at[ph]).wait()
-        pending.append((ph, ref))
+        pending.append(ref)
 
     def project(b, dst_q, dst_kv):
         t = tok_v[b]
@@ -170,7 +171,6 @@
     o_buf[...] = acc[0:128]
     s_xml[0:1] = m
     s_xml[1:2] = total
-
     def chunk(xp):
         return o_buf[pl.ds(pl.multiple_of(xp * 32, 32), 32)]
 
@@ -221,10 +221,12 @@
         [(m, total, part), (dm, dl, d_part)]
         + [(r_zml[i, 0:1], r_zml[i, 1:2], r_z2[i].astype(F32)) for i in range(NZ - 1)])
     att[c, x] = (part / total).astype(BF16)
-    for i in range(NX - 1):
-        send(14, att.at[c, x], att.at[c, x], x_dev[i])
+    for d in far_dev:
+        send(15, att.at[c, x], att.at[c, x], d)
+    for d in x_dev:
+        send(14, att.at[c, x], att.at[c, x], d)
+    send(15, att.at[c, x], att.at[c, x], core_peer)
     arrive(14, att.at[0, 0:NX - 1])
-    send(15, att.at[c], att.at[c], core_peer)
 
     def mix(b):
         a = att[b].reshape(128, 128).T
@@ -245,8 +247,8 @@
             ys = ys + r_y[i].astype(F32)
     out[...] = ys.T.astype(BF16).reshape(out.shape)
 
-    for ph, ref in pending:
-        pltpu.make_async_copy(ref, ref, send_sem.at[ph]).wait()
+    for ref in pending:
+        pltpu.make_async_copy(ref, ref, send_sem).wait()
 
 
 def per_device(NZ, NY, *args):
@@ -268,7 +270,7 @@
         V((32, 128), BF16), V((2, 128), F32), V((nz, 32, 128), BF16), V((nz, 2, 128), F32),
         V((128, 128), F32), V((2, 4, 32, 128), BF16), V((2, 16, 128), F32),
         V((NY, piece, 32), BF16), V((ny, piece, 32), BF16),
-        pltpu.SemaphoreType.DMA((8,)), pltpu.SemaphoreType.DMA((17,)), pltpu.SemaphoreType.DMA((17,)),
+        pltpu.SemaphoreType.DMA((8,)), pltpu.SemaphoreType.DMA, pltpu.SemaphoreType.DMA((17,)),
     ]
     return pl.pallas_call(
         functools.partial(kernel, NZ, NY),

time: 49 us -> 47.6 us (0.971)
  Pallas kernels: 47.4 us -> 46.1 us
    pallas_call x1, Pallas kernels: 47.4 us -> 46.1 us  [per_device(): pl.pallas_call(functools.partial(kernel, NZ, NY), out_shape=jax.ShapeDtyp...]
where the time goes in v4:
time: 47.6 us; the launch traced here: 47.4 us
  Pallas kernels  46.1 us (97%)
  local copies, waits for them, and re-layouts  1.3 us (3%)
    pallas_call x1, Pallas kernels, per_device(): pl.pallas_call(functools.partial(kernel, NZ, NY), out_shape=jax.ShapeDtyp...  46.1 us
    unnamed x1, local copies, waits for them, and re-layouts  1.3 us

profile of v4, /device:TPU:1, one launch (start us, length us, event | category | flops | bytes accessed | tf_op | source)
XLA Modules:
  0.0 47.4 jit_solution(2926646041345872485)
XLA Ops:
  0.0 46.1 %decode_step.1 = bf16[2,16,16]{2,1,0:T(8,128)(2,1)} custom-call(bf16[2,16,128]{2,1,0:T(8,128)(2,1)} %tok.1, bf16[128,1024]{1,0:T(8,128)(2,1)} %wq.1, bf16[128,128]{1,0:T(8,128)(2,1)} %wk.1, bf16[128,128]{1,0:T(8,128)(2,1)} %wv.1, bf16[2,1,2048,128]{3,2,1,0:T(8,128)(2,1)} %kc.1, bf16[2,1,2048,128]{3,2,1,0:T(8,128)(2,1)} %vc.1, s32[2]{0:T(128)} %ln.1, ...), custom_call_target="tpu_custom_call" | custom-call | tf_op jit(solution)/shard_map/decode_step/pallas_call | solution.py:275
  46.1 1.3 %copy.10 = bf16[2,16,16]{2,1,0:T(8,128)(2,1)} copy(bf16[2,16,16]{2,1,0:T(8,128)(2,1)} %decode_step.1) | data formatting | bytes 2048

commit v5 on v4

--- a/solution.py
+++ b/solution.py
@@ -22,7 +22,7 @@
            tok, wq, wk, wv, kc, vc, ln, wo, out,
            tok_v, wq_v, wk_v, wv_v, k_v, v_v, ln_s, wo_v, vt,
            p_oq, p_okv, p_cq, p_ckv, r_cq, r_ckv, s_zq, r_zq, s_xkv, r_xkv, r_xq, s_zkv, r_zkv, q_full, kv_full,
-           s_buf, o_buf, s_x2, s_xml, r_x2, r_xml, s_z2, s_zml, r_z2, r_zml,
+           bias, s_buf, o_buf, s_x2, s_xml, r_x2, r_xml, s_z2, s_zml, r_z2, r_zml,
            o_draft, att, y_buf, s_y, r_y,
            load_sem, send_sem, recv_sem):
     ctx, y = lax.axis_index("ctx"), lax.axis_index("head")
@@ -30,7 +30,7 @@
     x = lax.rem(ctx // 2, NX)
     z = ctx // (2 * NX)
     o = 1 - c
-    n_pos, hz = k_v.shape[1], 8 // NZ
+    n_pos, hz = v_v.shape[1], 8 // NZ
 
     core_peer = {"ctx": ctx + 1 - 2 * c}
     x_peers = [lax.rem(x + k, NX) for k in (2, 1, 3)]
@@ -42,7 +42,7 @@
     y_dev = [{"head": yp} for yp in y_peers]
 
     bar = pltpu.get_barrier_semaphore()
-    everyone = z_dev + y_dev + far_dev + x_dev + [core_peer]
+    everyone = z_dev + y_dev + x_dev + [core_peer]
     for d in everyone:
         pl.semaphore_signal(bar, inc=1, device_id=d, device_id_type=MESH)
 
@@ -56,7 +56,7 @@
     ld_wk = load(2, wk, wk_v)
     ld_wv = load(3, wv, wv_v)
     ld_v = load(4, vc.at[c, 0], v_v.at[0])
-    ld_k = load(5, kc.at[c, 0], k_v.at[0])
+    ld_k = load(5, kc.at[c, 0], k_v.at[0:n_pos])
     ld_wo = load(6, wo, wo_v)
     ld_ln = load(7, ln, ln_s)
 
@@ -104,7 +104,7 @@
     kvs = p_ckv[x] + r_ckv[x]
 
     send(8, vc.at[o, 0], v_v.at[1], core_peer)
-    send(9, kc.at[o, 0], k_v.at[1], core_peer)
+    send(9, kc.at[o, 0], k_v.at[n_pos:2 * n_pos], core_peer)
 
     if NZ > 1:
         arrive(2, r_zq)
@@ -142,31 +142,33 @@
             w = n_pos // 4
             vt[0:128, half * n_pos + w * i:half * n_pos + w * (i + 1)] = v_v[half, w * i:w * (i + 1)].T
 
+    ld_ln.wait()
+    for half in range(2):
+        live = ln_s[c] - (ctx + half * (1 - 2 * c)) * n_pos
+        at = lax.broadcasted_iota(jnp.int32, (n_pos, 128), 0)
+        bias[half * n_pos:(half + 1) * n_pos] = jnp.where(at < live, 0.0, NEG)
     ld_v.wait()
     transpose_values(0)
     arrive(8, v_v.at[0])
     transpose_values(1)
     ld_k.wait()
-    arrive(9, k_v.at[0])
-    ld_ln.wait()
+    arrive(9, k_v.at[0:n_pos])
     if NZ > 1:
         arrive(6, q_full.at[0:8 - hz])
 
     q = q_full[...].reshape(128, 128)
-    step = 512
-    steps = [(half, i) for half in range(2) for i in range(n_pos // step)]
     m = jnp.full((8, 128), NEG, F32)
-    for n, (half, i) in enumerate(steps):
-        s = dot_t(k_v[half, step * i:step * (i + 1)], q)
-        live = ln_s[c] - (ctx + half * (1 - 2 * c)) * n_pos - step * i
-        s = jnp.where(lax.broadcasted_iota(jnp.int32, (step, 128), 0) < live, s, NEG)
-        s_buf[step * n:step * (n + 1)] = s
-        m = jnp.maximum(m, jnp.max(s.reshape(step // 8, 8, 128), axis=0))
+    for n in range(2 * n_pos // 1024):
+        rows = slice(1024 * n, 1024 * (n + 1))
+        s = dot_t(k_v[rows], q) + bias[rows]
+        s_buf[rows] = s
+        m = jnp.maximum(m, jnp.max(s.reshape(1024 // 8, 8, 128), axis=0))
     m = jnp.max(m, axis=0, keepdims=True)
     acc = jnp.zeros((144, 128), F32)
-    for n in range(len(steps)):
-        w = jnp.exp(s_buf[step * n:step * (n + 1)] - m).astype(BF16)
-        acc = acc + jnp.dot(vt[:, step * n:step * (n + 1)], w, preferred_element_type=F32)
+    for n in range(2 * n_pos // 512):
+        rows = slice(512 * n, 512 * (n + 1))
+        w = jnp.exp(s_buf[rows] - m).astype(BF16)
+        acc = acc + jnp.dot(vt[:, rows], w, preferred_element_type=F32)
     total = acc[128:129]
     o_buf[...] = acc[0:128]
     s_xml[0:1] = m
@@ -258,14 +260,14 @@
     V = pltpu.VMEM
     scratch = [
         V(tok.shape, BF16), V(wq.shape, BF16), V(wk.shape, BF16), V(wv.shape, BF16),
-        V((2, n_pos, 128), BF16), V((2, n_pos, 128), BF16), pltpu.SMEM((2,), jnp.int32), V(wo.shape, BF16),
+        V((2 * n_pos, 128), BF16), V((2, n_pos, 128), BF16), pltpu.SMEM((2,), jnp.int32), V(wo.shape, BF16),
         V((144, 2 * n_pos), BF16),
         V((8, 16, 128), F32), V((4, 8, 128), F32), V((8, 16, 128), F32), V((4, 8, 128), F32),
         V((8, 16, 128), F32), V((4, 8, 128), F32),
         V((nz, hz, 16, 128), F32), V((nz, hz, 16, 128), F32), V((3, 8, 128), F32), V((3, 8, 128), F32),
         V((4, hz, 16, 128), F32), V((8, 128), F32), V((nz, 8, 128), F32),
         V((8, 16, 128), BF16), V((4, 8, 128), F32),
-        V((2 * n_pos, 128), F32), V((128, 128), F32),
+        V((2 * n_pos, 128), F32), V((2 * n_pos, 128), F32), V((128, 128), F32),
         V((3, 32, 128), BF16), V((2, 128), F32), V((3, 32, 128), BF16), V((3, 2, 128), F32),
         V((32, 128), BF16), V((2, 128), F32), V((nz, 32, 128), BF16), V((nz, 2, 128), F32),
         V((128, 128), F32), V((2, 4, 32, 128), BF16), V((2, 16, 128), F32),

time: 47.6 us -> 47.4 us (level)
  no operation moved by 1% of the time
where the time goes in v5:
time: 47.4 us; the launch traced here: 47.2 us
  Pallas kernels  45.9 us (97%)
  local copies, waits for them, and re-layouts  1.3 us (3%)
    pallas_call x1, Pallas kernels, per_device(): pl.pallas_call(functools.partial(kernel, NZ, NY), out_shape=jax.ShapeDtyp...  45.9 us
    unnamed x1, local copies, waits for them, and re-layouts  1.3 us

profile of v5, /device:TPU:1, one launch (start us, length us, event | category | flops | bytes accessed | tf_op | source)
XLA Modules:
  0.0 47.2 jit_solution(5281689794401662674)
XLA Ops:
  0.0 45.9 %decode_step.1 = bf16[2,16,16]{2,1,0:T(8,128)(2,1)} custom-call(bf16[2,16,128]{2,1,0:T(8,128)(2,1)} %tok.1, bf16[128,1024]{1,0:T(8,128)(2,1)} %wq.1, bf16[128,128]{1,0:T(8,128)(2,1)} %wk.1, bf16[128,128]{1,0:T(8,128)(2,1)} %wv.1, bf16[2,1,2048,128]{3,2,1,0:T(8,128)(2,1)} %kc.1, bf16[2,1,2048,128]{3,2,1,0:T(8,128)(2,1)} %vc.1, s32[2]{0:T(128)} %ln.1, ...), custom_call_target="tpu_custom_call" | custom-call | tf_op jit(solution)/shard_map/decode_step/pallas_call | solution.py:277
  45.9 1.3 %copy.10 = bf16[2,16,16]{2,1,0:T(8,128)(2,1)} copy(bf16[2,16,16]{2,1,0:T(8,128)(2,1)} %decode_step.1) | data formatting | bytes 2048
